TPU v7x, 512 devices: a whole 4x8x8 slice. The times are simulated.
512 devices in a mesh: dp: 32 (over z, y_hi, core), tensor: 4 (over y_lo), replica: 4 (over x).
Axes of the slice: x: 4, y: 8 (y_hi: 2, y_lo: 4; y = y_hi * 4 + y_lo), z: 8, core: 2. Of those that a mesh axis runs over, the one named last changes fastest.
Arguments:
- acts: bfloat16 [32768, 5120], P(('dp', 'replica'), 'tensor'), may hold values from -64 to 64
- out_grads: bfloat16 [32768, 5120], P(('dp', 'replica'), 'tensor'), may hold values from -64 to 64
- grad_parts: bfloat16 [4, 5120, 5120], P('replica', 'dp', 'tensor'), may hold values from -24 to 24
- basis_a: bfloat16 [40, 128, 128], P('tensor'), may hold values from -0.5 to 0.5
- basis_g: bfloat16 [40, 128, 128], P('tensor'), may hold values from -0.5 to 0.5
- fac_old: float32 [4, 32, 128, 128], P('tensor', 'dp'), as said below
- owner_slot: int32 [4, 20], replicated, may hold values from 0 to 31, as said below
Outputs:
- update: bfloat16 [5120, 5120], P('dp', 'tensor')
- fac_new: float32 [4, 32, 128, 128], P('tensor', 'dp')
Inputs may be any that keep to these rules, and one draw needn't show every extreme that they name: `owner_slot`: each row names 20 different slots; slot s belongs to owner s // 1 on dp; in each row some owner holds 1 factors. `fac_old`: each block is symmetric positive definite.
All inputs are finite; a program needn't handle non-finite values.
Results may differ from a plain program's by a relative error of at most 0.019.
Values may be sent and summed in bfloat16 or wider, within the bound.
A program may use at most 64 MiB of HBM per device.

v0:
```python
import jax
import jax.numpy as jnp
from jax import lax
from jax.experimental import pallas as pl
from jax.experimental.pallas import tpu as pltpu
from jax.sharding import PartitionSpec as P

MESH = pl.DeviceIdType.MESH
F32, BF16 = jnp.float32, jnp.bfloat16

DECAY = 0.5
DAMPING = 0.01
TOKENS = 32768
BLK = 128
HEADS = 10
FACTORS = 2 * HEADS
ROWS = 160
WIN = 2 * BLK
SLOTS = 32
Z, R = 8, 4
QR = BLK // R
X_ORDER = (2, 1, 3)
Z_ORDER = (4, 3, 5, 2, 6, 1, 7)
PAIRS = Z_ORDER + (0,)
PART = SLOTS // 4


def contract(a, b, da, db):
    return lax.dot_general(a, b, (((da,), (db,)), ((), ())), preferred_element_type=F32)


def kernel(
    owner, acts_hbm, grads_hbm, parts_hbm, qa_hbm, qg_hbm, fac_hbm,
    update_hbm, fac_out,
    acts, outg, part, bases, fac, gwin, cov, slot_f, slot_u,
    v0_send, v0_recv, v1_buf, v1_recv, v2_send, v2_recv, vy_send, vy_recv, v3_buf,
    e_part, e1_buf, e2_buf, e3_send, ei_buf, eo_buf,
    m1a, m1b, turned, win, back, upd,
    local_sem, m1a_s, m1a_r, m1b_s, m1b_r, g_s, g_r, v0_s, v0_r, v1_s, v1_r, v2_s, v2_r, vy_s, vy_r,
    v3_s, v3_r, e1_s, e1_r, e2_s, e2_r, ei_s, ei_r, eo_s, eo_r, m2_s, m2_r, m3_s, m3_r,
):
    d = lax.axis_index("dp")
    t = lax.axis_index("tensor")
    r = lax.axis_index("replica")
    z, q = d // 4, d % 4
    yh, c = q // 2, q % 2
    home_t = z // 2
    half = z % 2

    def at(zz, yy, cc, tt, rr):
        return (zz * 4 + yy * 2 + cc, tt, rr)

    me_dev = at(z, yh, c, t, r)

    def remote(src, dst, s, rcv, dev):
        return pltpu.make_async_remote_copy(
            src_ref=src, dst_ref=dst, send_sem=s, recv_sem=rcv, device_id=dev, device_id_type=MESH
        )

    def arrived(dst, rcv, s):
        remote(dst, dst, s, rcv, me_dev).wait_recv()

    def first_block(rr):
        return (5 * rr + 1) // 2

    loads = [
        pltpu.make_async_copy(acts_hbm, acts, local_sem.at[0]),
        pltpu.make_async_copy(grads_hbm, outg, local_sem.at[1]),
        pltpu.make_async_copy(qa_hbm, bases.at[pl.ds(0, HEADS)], local_sem.at[2]),
        pltpu.make_async_copy(qg_hbm, bases.at[pl.ds(HEADS, HEADS)], local_sem.at[3]),
        pltpu.make_async_copy(fac_hbm, fac, local_sem.at[4]),
        pltpu.make_async_copy(parts_hbm, part, local_sem.at[5]),
    ]
    for cp in loads:
        cp.start()

    peers = []
    for k in range(1, R):
        for j in range(2):
            peers.append(at(z, yh, (c + j) % 2, t, (r + k) % R))
    for k in range(4):
        for j in range(2):
            for i in range(2):
                if k or j or i:
                    peers.append(at(z, (yh + j) % 2, (c + i) % 2, (t + k) % 4, r))
    for k in range(1, Z):
        peers.append(at((z + k) % Z, yh, c, t, r))
    barrier = pltpu.get_barrier_semaphore()
    for dev in peers:
        pl.semaphore_signal(barrier, inc=1, device_id=dev, device_id_type=MESH)

    def lookup(s, carry):
        f, u = jnp.int32(0), jnp.int32(0)
        for k in range(FACTORS):
            hit = owner[t, k] == s
            f, u = jnp.where(hit, k, f), jnp.where(hit, 1, u)
        slot_f[s] = f
        slot_u[s] = u
        return carry

    lax.fori_loop(0, SLOTS, lookup, 0)

    for side in range(2):
        src = acts if side == 0 else outg
        loads[side].wait()
        for b in range(HEADS):
            a = src[:, b * BLK:(b + 1) * BLK]
            cov[side * HEADS + b] = contract(a, a, 0, 0)

    def pick(s):
        return cov[slot_f[s]] * slot_u[s].astype(F32)

    def slot(j, core):
        return (z + PAIRS[j // 2]) % Z * 4 + j % 2 * 2 + core

    for j in range(SLOTS // 2):
        v0_send[j] = pick(slot(j, 1 - c)).astype(BF16)

    loads[2].wait()
    loads[3].wait()
    loads[4].wait()
    e_part[...] = jnp.zeros_like(e_part)
    for f in range(FACTORS):
        src = acts if f < HEADS else outg
        b = f % HEADS
        rot = contract(src[:, b * BLK:(b + 1) * BLK], bases[f], 1, 0)
        at_row = f if f < HEADS else (f + 6 if f < 15 else f + 9)
        e_part[at_row:at_row + 1, :] = jnp.sum(rot * rot, axis=0, keepdims=True) * (DECAY / TOKENS)
    own_f = slot_f[d]
    own_u = slot_u[d].astype(F32)
    own_q = bases[own_f]
    old = fac[...]
    hi = old.astype(BF16)
    rest = old - hi.astype(F32)
    mid = rest.astype(BF16)
    low = (rest - mid.astype(F32)).astype(BF16)
    fq = contract(hi, own_q, 1, 0) + contract(mid, own_q, 1, 0) + contract(low, own_q, 1, 0)
    diag = jnp.sum(own_q.astype(F32) * fq, axis=0, keepdims=True)
    place = own_f + jnp.where(own_f >= 10, 6, 0) + jnp.where(own_f >= 15, 3, 0)
    share = DECAY * own_u * (r == 0).astype(F32)
    rows = lax.broadcasted_iota(jnp.int32, (SLOTS, BLK), 0)
    e_part[...] += jnp.where(rows == place, diag * share, 0.0)

    pl.semaphore_wait(barrier, len(peers))

    v0 = []
    for h in range(2):
        part_h = pl.ds(h * PART, PART)
        v0.append(remote(v0_send.at[part_h], v0_recv.at[part_h], v0_s.at[h], v0_r.at[h], at(z, yh, 1 - c, t, r)))
        v0[-1].start()

    e1 = []
    own8 = 2 * r + c
    for k in range(1, 8):
        to = (own8 + k) % 8
        rows_to = pl.ds(pl.multiple_of(16 * (to % 2), 16), 16)
        e1.append(remote(e_part.at[rows_to], e1_buf.at[own8], e1_s.at[k], e1_r.at[own8], at(z, yh, to % 2, t, to // 2)))
        e1[-1].start()

    m1 = []
    for k in range(1, R):
        rr = (r + k) % R
        first = pl.multiple_of(first_block(rr) * BLK, BLK)
        m1.append(remote(parts_hbm.at[:, pl.ds(first, 2 * BLK)], m1a.at[r], m1a_s.at[k], m1a_r.at[r], at(z, yh, c, t, rr)))
        m1[-1].start()

        @pl.when(rr % 2 == 0)
        def _():
            third = pl.multiple_of((first_block(rr) + 2) * BLK, BLK)
            remote(parts_hbm.at[:, pl.ds(third, BLK)], m1b.at[r], m1b_s.at[k], m1b_r.at[r], at(z, yh, c, t, rr)).start()

    @pl.when(t == home_t)
    def _():
        for k in range(1, 4):
            remote(qg_hbm.at[pl.ds(5 * half + q, 2)], gwin, g_s.at[k], g_r, at(z, yh, c, (t + k) % 4, r)).start()
        pltpu.make_async_copy(qg_hbm.at[pl.ds(5 * half + q, 2)], gwin, local_sem.at[6]).start()

    v1 = []
    for h in range(2):
        v0[h].wait_recv()
        for j in range(h * PART, (h + 1) * PART):
            both = (pick(slot(j, c)) + v0_recv[j].astype(F32)).astype(BF16)
            for i in range(R):
                v1_buf[i, j] = both[i * QR:(i + 1) * QR]
        part_h = pl.ds(h * PART, PART)
        for k in X_ORDER:
            rr = (r + k) % R
            v1.append(remote(
                v1_buf.at[rr, part_h], v1_recv.at[r, part_h],
                v1_s.at[h, k], v1_r.at[h, r], at(z, yh, c, t, rr),
            ))
            v1[-1].start()

    total = e_part[pl.ds(pl.multiple_of(16 * c, 16), 16), :]
    for k in range(1, 8):
        frm = (own8 + k) % 8
        arrived(e1_buf.at[frm], e1_r.at[frm], e1_s.at[0])
        total += e1_buf[frm]
    e2_buf[z] = total
    e2 = []
    for k in Z_ORDER:
        e2.append(remote(e2_buf.at[z], e2_buf.at[z], e2_s.at[k], e2_r.at[z], at((z + k) % Z, yh, c, t, r)))
        e2[-1].start()

    loads[5].wait()
    for k in range(1, R):
        rr = (r + k) % R
        arrived(m1a.at[rr], m1a_r.at[rr], m1a_s.at[0])

        @pl.when(r % 2 == 0)
        def _():
            arrived(m1b.at[rr], m1b_r.at[rr], m1b_s.at[0])

    first = first_block(r)
    ids = [first, first + 1, jnp.minimum(first + 2, HEADS - 1)]
    for j in range(3):
        grad = part[:, pl.ds(pl.multiple_of(ids[j] * BLK, BLK), BLK)].astype(F32)
        for k in range(1, R):
            rr = (r + k) % R
            if j < 2:
                grad += m1a[rr, :, j * BLK:(j + 1) * BLK].astype(F32)
            else:
                grad += m1b[rr].astype(F32)
        turned[:, j * BLK:(j + 1) * BLK] = contract(grad.astype(BF16), bases[ids[j]], 1, 0).astype(BF16)

    halo = {
        0: [(128, 32, 0, 1)],
        1: [(0, 96, 160, 0), (96, 64, 0, 2)],
        2: [(64, 96, 0, 3), (0, 64, 192, 1)],
        3: [(0, 32, 224, 2)],
    }

    def halo_copies(me):
        out = []
        for i, (row, n, to_row, to) in enumerate(halo[me]):
            out.append(remote(
                turned.at[pl.ds(row, n)], win.at[pl.ds(to_row, n)],
                m2_s.at[i], m2_r.at[i], at(z, to // 2, to % 2, t, r),
            ))
        return out

    for me in range(4):
        @pl.when(q == me)
        def _():
            for cp in halo_copies(me):
                cp.start()

    win[pl.ds(pl.multiple_of(32 * q, 32), ROWS), :] = turned[...]

    total = e2_buf[z]
    for k in range(1, Z):
        zz = (z + k) % Z
        arrived(e2_buf.at[zz], e2_r.at[zz], e2_s.at[0])
        total += e2_buf[zz]
    e3_send[...] = total
    out_rows = pl.ds(pl.multiple_of(8 * half, 8), 8)

    def share_in(k):
        y_to, c_to = (yh + k // 2) % 2, k % 2
        return remote(e3_send, ei_buf.at[yh], ei_s.at[k], ei_r.at[yh], at(z, y_to, c_to, t, r))

    def share_out(k):
        y_to, c_to, t_to = (yh + (k // 2) % 2) % 2, (1 + k) % 2, (t + k // 4) % 4
        return remote(e3_send.at[out_rows], eo_buf.at[yh], eo_s.at[k], eo_r.at[yh], at(z, y_to, c_to, t_to, r))

    @pl.when(c == 0)
    def _():
        for k in range(1, 4):
            share_in(k).start()
        ei_buf[yh] = e3_send[...]

    @pl.when((c == 1) & (t == home_t))
    def _():
        for k in range(1, 16):
            share_out(k).start()
        eo_buf[yh] = e3_send[out_rows, :]

    v2 = []
    for h in range(2):
        part_h = pl.ds(h * PART, PART)
        for k in range(1, R):
            rr = (r + k) % R
            arrived(v1_recv.at[rr, part_h], v1_r.at[h, rr], v1_s.at[h, 0])
        for j in range(h * PART, (h + 1) * PART):
            acc = v1_buf[r, j].astype(F32)
            for k in range(1, R):
                acc += v1_recv[(r + k) % R, j].astype(F32)
            v2_send[j] = acc.astype(BF16)
        for p in range(h * PART // 2, (h + 1) * PART // 2):
            if PAIRS[p]:
                v2.append(remote(
                    v2_send.at[pl.ds(2 * p, 2)], v2_recv.at[z],
                    v2_s.at[p], v2_r.at[z], at((z + PAIRS[p]) % Z, yh, c, t, r),
                ))
                v2[-1].start()

    def halo_arrivals(me):
        for src in range(4):
            for i, (row, n, to_row, to) in enumerate(halo[src]):
                if to == me:
                    arrived(win.at[pl.ds(to_row, n)], m2_r.at[i], m2_s.at[0])

    for me in range(4):
        @pl.when(q == me)
        def _():
            halo_arrivals(me)

    @pl.when(t == home_t)
    def _():
        pltpu.make_async_copy(qg_hbm.at[pl.ds(5 * half + q, 2)], gwin, local_sem.at[6]).wait()

    @pl.when(t != home_t)
    def _():
        arrived(gwin, g_r, g_s.at[0])

    inner = [contract(gwin[b], win[b * BLK:(b + 1) * BLK, :], 0, 0) for b in range(2)]

    @pl.when(c == 1)
    def _():
        arrived(ei_buf.at[yh], ei_r.at[yh], ei_s.at[0])

    @pl.when((c == 0) | (t != home_t))
    def _():
        arrived(eo_buf.at[yh], eo_r.at[yh], eo_s.at[0])

    arrived(ei_buf.at[1 - yh], ei_r.at[1 - yh], ei_s.at[0])
    arrived(eo_buf.at[1 - yh], eo_r.at[1 - yh], eo_s.at[0])

    eig_cols = []
    for b in range(2):
        row = pl.ds(q + b, 1)
        eig_out = eo_buf[0, row, :] + eo_buf[1, row, :]
        eig_cols.append(jnp.transpose(jnp.broadcast_to(eig_out, (BLK, BLK))))

    def block_at(j, rr):
        return pl.ds(pl.multiple_of((first_block(rr) + j) * BLK, BLK), BLK)

    def m3(j, k):
        return remote(upd.at[j], update_hbm.at[:, block_at(j, r)], m3_s.at[j, k], m3_r.at[j, r], at(z, yh, c, t, (r + k) % R))

    def own_block(j):
        return pltpu.make_async_copy(upd.at[j], update_hbm.at[:, block_at(j, r)], local_sem.at[7 + j])

    def send_block(j):
        for k in X_ORDER:
            m3(j, k).start()
        own_block(j).start()

    for j in range(3):
        cols = slice(j * BLK, (j + 1) * BLK)
        row_j = pl.ds(ids[j], 1)
        eig_in = ei_buf[0, row_j, :] + ei_buf[1, row_j, :]
        for b in range(2):
            scaled = (inner[b][:, cols] / (eig_cols[b] * eig_in + DAMPING)).astype(BF16)
            back[b * BLK:(b + 1) * BLK, :] = contract(gwin[b], scaled, 1, 0).astype(BF16)
        own_rows = back[pl.ds(pl.multiple_of(32 * q, 32), ROWS), :]
        upd[j] = contract(own_rows, bases[ids[j]], 1, 1).astype(BF16)
        if j < 2:
            send_block(j)
        else:
            pl.when(r % 2 == 0)(lambda: send_block(2))

    for k in range(1, Z):
        zz = (z + k) % Z
        arrived(v2_recv.at[zz], v2_r.at[zz], v2_s.at[0])

    def over_z(y):
        acc = v2_send[2 * (Z - 1) + y].astype(F32)
        for k in range(1, Z):
            acc += v2_recv[(z + k) % Z, y].astype(F32)
        return acc

    vy_send[...] = over_z(1 - yh).astype(BF16)
    vy = remote(vy_send, vy_recv, vy_s, vy_r, at(z, 1 - yh, c, t, r))
    vy.start()
    kept = over_z(yh)
    vy.wait_recv()
    v3_buf[r] = (kept + vy_recv[...].astype(F32)).astype(BF16)
    v3 = []
    for k in X_ORDER:
        v3.append(remote(v3_buf.at[r], v3_buf.at[r], v3_s.at[k], v3_r.at[r], at(z, yh, c, t, (r + k) % R)))
        v3[-1].start()
    for k in range(1, R):
        rr = (r + k) % R
        arrived(v3_buf.at[rr], v3_r.at[rr], v3_s.at[0])
    for i in range(R):
        old_rows = fac[i * QR:(i + 1) * QR, :]
        refreshed = DECAY * old_rows + (1.0 - DECAY) * (v3_buf[i].astype(F32) * (1.0 / TOKENS))
        fac_out[i * QR:(i + 1) * QR, :] = jnp.where(own_u > 0.0, refreshed, old_rows)

    for j in range(2):
        own_block(j).wait()
    for k in range(1, R):
        rr = (r + k) % R
        for j in range(2):
            arrived(update_hbm.at[:, block_at(j, rr)], m3_r.at[j, rr], m3_s.at[j, 0])

        @pl.when(rr % 2 == 0)
        def _():
            arrived(update_hbm.at[:, block_at(2, rr)], m3_r.at[2, rr], m3_s.at[2, 0])

    for k in range(1, R):
        m1[k - 1].wait_send()
        for j in range(2):
            m3(j, k).wait_send()

        @pl.when((r + k) % 2 == 0)
        def _():
            remote(m1b.at[0], m1b.at[0], m1b_s.at[k], m1b_r.at[0], me_dev).wait_send()

    @pl.when(r % 2 == 0)
    def _():
        for k in range(1, R):
            m3(2, k).wait_send()
        own_block(2).wait()

    @pl.when(t == home_t)
    def _():
        for k in range(1, 4):
            remote(gwin, gwin, g_s.at[k], g_r, me_dev).wait_send()

    @pl.when(c == 0)
    def _():
        for k in range(1, 4):
            share_in(k).wait_send()

    @pl.when((c == 1) & (t == home_t))
    def _():
        for k in range(1, 16):
            share_out(k).wait_send()

    for cp in v0 + e1 + e2 + v1 + v2 + [vy] + v3:
        cp.wait_send()
    for me in range(4):
        @pl.when(q == me)
        def _():
            for cp in halo_copies(me):
                cp.wait_send()


def place(update_in, fac_in, update_out, fac_new, held, held_fac, in_sem, out_sem):
    rows = ROWS // 5
    steps = [(fac_in, held_fac, fac_new)]
    for i in range(5):
        at = pl.ds(i * rows, rows)
        steps.append((update_in.at[at], held.at[at], update_out.at[at]))
    come = [pltpu.make_async_copy(src, mid, in_sem.at[i]) for i, (src, mid, _) in enumerate(steps)]
    go = [pltpu.make_async_copy(mid, dst, out_sem.at[i]) for i, (_, mid, dst) in enumerate(steps)]
    for cp in come:
        cp.start()
    for arrive, leave in zip(come, go):
        arrive.wait()
        leave.start()
    for cp in go:
        cp.wait()


def per_device(acts, out_grads, grad_parts, basis_a, basis_g, fac_old, owner_slot):
    sem = pltpu.SemaphoreType.DMA
    half_slots = SLOTS // 2
    hbm = pl.BlockSpec(memory_space=pl.ANY)
    update, fac_new = pl.pallas_call(
        kernel,
        out_shape=(
            jax.ShapeDtypeStruct((ROWS, HEADS * BLK), BF16),
            jax.ShapeDtypeStruct((BLK, BLK), F32),
        ),
        in_specs=[pl.BlockSpec(memory_space=pltpu.SMEM)] + [hbm] * 6,
        out_specs=(hbm, pl.BlockSpec(memory_space=pltpu.VMEM)),
        scratch_shapes=[
            pltpu.VMEM((256, HEADS * BLK), BF16),
            pltpu.VMEM((256, HEADS * BLK), BF16),
            pltpu.VMEM((ROWS, HEADS * BLK), BF16),
            pltpu.VMEM((FACTORS, BLK, BLK), BF16),
            pltpu.VMEM((BLK, BLK), F32),
            pltpu.VMEM((2, BLK, BLK), BF16),
            pltpu.VMEM((FACTORS, BLK, BLK), F32),
            pltpu.SMEM((SLOTS,), jnp.int32),
            pltpu.SMEM((SLOTS,), jnp.int32),
            pltpu.VMEM((half_slots, BLK, BLK), BF16),
            pltpu.VMEM((half_slots, BLK, BLK), BF16),
            pltpu.VMEM((R, half_slots, QR, BLK), BF16),
            pltpu.VMEM((R, half_slots, QR, BLK), BF16),
            pltpu.VMEM((half_slots, QR, BLK), BF16),
            pltpu.VMEM((Z, 2, QR, BLK), BF16),
            pltpu.VMEM((QR, BLK), BF16),
            pltpu.VMEM((QR, BLK), BF16),
            pltpu.VMEM((R, QR, BLK), BF16),
            pltpu.VMEM((SLOTS, BLK), F32),
            pltpu.VMEM((8, 16, BLK), F32),
            pltpu.VMEM((Z, 16, BLK), F32),
            pltpu.VMEM((16, BLK), F32),
            pltpu.VMEM((2, 16, BLK), F32),
            pltpu.VMEM((2, 8, BLK), F32),
            pltpu.VMEM((R, ROWS, 2 * BLK), BF16),
            pltpu.VMEM((R, ROWS, BLK), BF16),
            pltpu.VMEM((ROWS, 3 * BLK), BF16),
            pltpu.VMEM((WIN, 3 * BLK), BF16),
            pltpu.VMEM((WIN, BLK), BF16),
            pltpu.VMEM((3, ROWS, BLK), BF16),
            sem((10,)),
            sem((R,)), sem((R,)), sem((R,)), sem((R,)),
            sem((4,)), sem,
            sem((2,)), sem((2,)),
            sem((2, R)), sem((2, R)),
            sem((Z,)), sem((Z,)),
            sem, sem,
            sem((R,)), sem((R,)),
            sem((8,)), sem((8,)),
            sem((Z,)), sem((Z,)),
            sem((4,)), sem((2,)),
            sem((16,)), sem((2,)),
            sem((2,)), sem((2,)),
            sem((3, R)), sem((3, R)),
        ],
        compiler_params=pltpu.CompilerParams(
            collective_id=0, has_side_effects=True, vmem_limit_bytes=60 * 1024 * 1024
        ),
    )(owner_slot, acts, out_grads, grad_parts[0], basis_a, basis_g, fac_old[0, 0])
    update, fac_new = pl.pallas_call(
        place,
        out_shape=(jax.ShapeDtypeStruct(update.shape, BF16), jax.ShapeDtypeStruct(fac_new.shape, F32)),
        in_specs=[hbm, hbm],
        out_specs=(hbm, hbm),
        scratch_shapes=[pltpu.VMEM(update.shape, BF16), pltpu.VMEM(fac_new.shape, F32), sem((6,)), sem((6,))],
        compiler_params=pltpu.CompilerParams(vmem_limit_bytes=60 * 1024 * 1024),
    )(update, fac_new)
    return update, fac_new[None, None]


def solution(mesh):
    placed = (
        P(("dp", "replica"), "tensor"),
        P(("dp", "replica"), "tensor"),
        P("replica", "dp", "tensor"),
        P("tensor", None, None),
        P("tensor", None, None),
        P("tensor", "dp", None, None),
        P(),
    )
    return jax.shard_map(
        per_device,
        mesh=mesh,
        in_specs=placed,
        out_specs=(P("dp", "tensor"), P("tensor", "dp", None, None)),
        check_vma=False,
    )
```

profile of v0, /device:TPU:2, one launch (start us, length us, event | category | flops | bytes accessed | tf_op | source)
XLA Modules:
  0.0 44.9 jit_solution(12026591555504365808)
XLA Ops:
  0.6 42.5 %shard_map.86 = (bf16[160,1280]{1,0:T(8,128)(2,1)}, f32[128,128]{1,0:T(8,128)}) custom-call(s32[4,20]{1,0:T(4,128)} %owner.1, bf16[256,1280]{1,0:T(8,128)(2,1)} %acts_hbm.1, bf16[256,1280]{1,0:T(8,128)(2,1)} %grads_hbm.1, bf16[160,1280]{1,0:T(8,128)(2,1)} %bitcast.3, bf16[10,128,128]{2,1,0:T(8,128)(2,1)} %qa_hbm.1, bf16[10,128,128]{2,1,0:T(8,128)(2,1)} %qg_hbm.1, ...), custom_call_target="tpu_custom_call" | custom-call | tf_op jit(solution)/shard_map/pallas_call | solution.py:462
  43.1 1.8 %shard_map.87 = (bf16[160,1280]{1,0:T(8,128)(2,1)}, f32[128,128]{1,0:T(8,128)}) custom-call(bf16[160,1280]{1,0:T(8,128)(2,1)} %get-tuple-element.6.update_in, f32[128,128]{1,0:T(8,128)} %get-tuple-element.7.fac_in), custom_call_target="tpu_custom_call" | custom-call | tf_op jit(solution)/shard_map/pallas_call | solution.py:520
where the time goes:
time: 45.1 us; the launch traced here: 44.9 us
  Pallas kernels  44.3 us (98%)
  between operations  0.64 us (1%)
    pallas_call x1, Pallas kernels, per_device(): pl.pallas_call(kernel, out_shape=(jax.ShapeDtypeStruct((ROWS, HEADS * BLK...  42.5 us
    pallas_call x1, Pallas kernels, per_device(): pl.pallas_call(place, out_shape=(jax.ShapeDtypeStruct(update.shape, BF16)...  1.82 us

commit v1 on v0

--- a/solution.py
+++ b/solution.py
@@ -63,19 +63,8 @@
     def first_block(rr):
         return (5 * rr + 1) // 2
 
-    loads = [
-        pltpu.make_async_copy(acts_hbm, acts, local_sem.at[0]),
-        pltpu.make_async_copy(grads_hbm, outg, local_sem.at[1]),
-        pltpu.make_async_copy(qa_hbm, bases.at[pl.ds(0, HEADS)], local_sem.at[2]),
-        pltpu.make_async_copy(qg_hbm, bases.at[pl.ds(HEADS, HEADS)], local_sem.at[3]),
-        pltpu.make_async_copy(fac_hbm, fac, local_sem.at[4]),
-        pltpu.make_async_copy(parts_hbm, part, local_sem.at[5]),
-    ]
-    for cp in loads:
-        cp.start()
-
     peers = []
-    for k in range(1, R):
+    for k in X_ORDER:
         for j in range(2):
             peers.append(at(z, yh, (c + j) % 2, t, (r + k) % R))
     for k in range(4):
@@ -88,6 +77,17 @@
     barrier = pltpu.get_barrier_semaphore()
     for dev in peers:
         pl.semaphore_signal(barrier, inc=1, device_id=dev, device_id_type=MESH)
+
+    loads = [
+        pltpu.make_async_copy(acts_hbm, acts, local_sem.at[0]),
+        pltpu.make_async_copy(grads_hbm, outg, local_sem.at[1]),
+        pltpu.make_async_copy(qa_hbm, bases.at[pl.ds(0, HEADS)], local_sem.at[2]),
+        pltpu.make_async_copy(qg_hbm, bases.at[pl.ds(HEADS, HEADS)], local_sem.at[3]),
+        pltpu.make_async_copy(fac_hbm, fac, local_sem.at[4]),
+        pltpu.make_async_copy(parts_hbm, part, local_sem.at[5]),
+    ]
+    for cp in loads:
+        cp.start()
 
     def lookup(s, carry):
         f, u = jnp.int32(0), jnp.int32(0)
@@ -143,12 +143,6 @@
 
     pl.semaphore_wait(barrier, len(peers))
 
-    v0 = []
-    for h in range(2):
-        part_h = pl.ds(h * PART, PART)
-        v0.append(remote(v0_send.at[part_h], v0_recv.at[part_h], v0_s.at[h], v0_r.at[h], at(z, yh, 1 - c, t, r)))
-        v0[-1].start()
-
     e1 = []
     own8 = 2 * r + c
     for k in range(1, 8):
@@ -157,6 +151,12 @@
         e1.append(remote(e_part.at[rows_to], e1_buf.at[own8], e1_s.at[k], e1_r.at[own8], at(z, yh, to % 2, t, to // 2)))
         e1[-1].start()
 
+    v0 = []
+    for h in range(2):
+        part_h = pl.ds(h * PART, PART)
+        v0.append(remote(v0_send.at[part_h], v0_recv.at[part_h], v0_s.at[h], v0_r.at[h], at(z, yh, 1 - c, t, r)))
+        v0[-1].start()
+
     m1 = []
     for k in range(1, R):
         rr = (r + k) % R
@@ -168,12 +168,6 @@
         def _():
             third = pl.multiple_of((first_block(rr) + 2) * BLK, BLK)
             remote(parts_hbm.at[:, pl.ds(third, BLK)], m1b.at[r], m1b_s.at[k], m1b_r.at[r], at(z, yh, c, t, rr)).start()
-
-    @pl.when(t == home_t)
-    def _():
-        for k in range(1, 4):
-            remote(qg_hbm.at[pl.ds(5 * half + q, 2)], gwin, g_s.at[k], g_r, at(z, yh, c, (t + k) % 4, r)).start()
-        pltpu.make_async_copy(qg_hbm.at[pl.ds(5 * half + q, 2)], gwin, local_sem.at[6]).start()
 
     v1 = []
     for h in range(2):
@@ -191,6 +185,12 @@
             ))
             v1[-1].start()
 
+    @pl.when(t == home_t)
+    def _():
+        for k in range(1, 4):
+            remote(qg_hbm.at[pl.ds(5 * half + q, 2)], gwin, g_s.at[k], g_r, at(z, yh, c, (t + k) % 4, r)).start()
+        pltpu.make_async_copy(qg_hbm.at[pl.ds(5 * half + q, 2)], gwin, local_sem.at[6]).start()
+
     total = e_part[pl.ds(pl.multiple_of(16 * c, 16), 16), :]
     for k in range(1, 8):
         frm = (own8 + k) % 8
@@ -201,6 +201,34 @@
     for k in Z_ORDER:
         e2.append(remote(e2_buf.at[z], e2_buf.at[z], e2_s.at[k], e2_r.at[z], at((z + k) % Z, yh, c, t, r)))
         e2[-1].start()
+
+    total = e2_buf[z]
+    for k in range(1, Z):
+        zz = (z + k) % Z
+        arrived(e2_buf.at[zz], e2_r.at[zz], e2_s.at[0])
+        total += e2_buf[zz]
+    e3_send[...] = total
+    out_rows = pl.ds(pl.multiple_of(8 * half, 8), 8)
+
+    def share_in(k):
+        y_to, c_to = (yh + k // 2) % 2, k % 2
+        return remote(e3_send, ei_buf.at[yh], ei_s.at[k], ei_r.at[yh], at(z, y_to, c_to, t, r))
+
+    def share_out(k):
+        y_to, c_to, t_to = (yh + (k // 2) % 2) % 2, (1 + k) % 2, (t + k // 4) % 4
+        return remote(e3_send.at[out_rows], eo_buf.at[yh], eo_s.at[k], eo_r.at[yh], at(z, y_to, c_to, t_to, r))
+
+    @pl.when(c == 0)
+    def _():
+        for k in range(1, 4):
+            share_in(k).start()
+        ei_buf[yh] = e3_send[...]
+
+    @pl.when((c == 1) & (t == home_t))
+    def _():
+        for k in range(1, 16):
+            share_out(k).start()
+        eo_buf[yh] = e3_send[out_rows, :]
 
     loads[5].wait()
     for k in range(1, R):
@@ -246,34 +274,6 @@
                 cp.start()
 
     win[pl.ds(pl.multiple_of(32 * q, 32), ROWS), :] = turned[...]
-
-    total = e2_buf[z]
-    for k in range(1, Z):
-        zz = (z + k) % Z
-        arrived(e2_buf.at[zz], e2_r.at[zz], e2_s.at[0])
-        total += e2_buf[zz]
-    e3_send[...] = total
-    out_rows = pl.ds(pl.multiple_of(8 * half, 8), 8)
-
-    def share_in(k):
-        y_to, c_to = (yh + k // 2) % 2, k % 2
-        return remote(e3_send, ei_buf.at[yh], ei_s.at[k], ei_r.at[yh], at(z, y_to, c_to, t, r))
-
-    def share_out(k):
-        y_to, c_to, t_to = (yh + (k // 2) % 2) % 2, (1 + k) % 2, (t + k // 4) % 4
-        return remote(e3_send.at[out_rows], eo_buf.at[yh], eo_s.at[k], eo_r.at[yh], at(z, y_to, c_to, t_to, r))
-
-    @pl.when(c == 0)
-    def _():
-        for k in range(1, 4):
-            share_in(k).start()
-        ei_buf[yh] = e3_send[...]
-
-    @pl.when((c == 1) & (t == home_t))
-    def _():
-        for k in range(1, 16):
-            share_out(k).start()
-        eo_buf[yh] = e3_send[out_rows, :]
 
     v2 = []
     for h in range(2):

time: 45.1 us -> 45.1 us (level)
  no operation moved by 1% of the time
where the time goes in v1:
time: 45.1 us; the launch traced here: 44.9 us
  Pallas kernels  44.3 us (98%)
  between operations  0.64 us (1%)
    pallas_call x1, Pallas kernels, per_device(): pl.pallas_call(kernel, out_shape=(jax.ShapeDtypeStruct((ROWS, HEADS * BLK...  42.5 us
    pallas_call x1, Pallas kernels, per_device(): pl.pallas_call(place, out_shape=(jax.ShapeDtypeStruct(update.shape, BF16)...  1.82 us

profile of v1, /device:TPU:2, one launch (start us, length us, event | category | flops | bytes accessed | tf_op | source)
XLA Modules:
  0.0 44.9 jit_solution(1830744467392155984)
XLA Ops:
  0.6 42.5 %shard_map.86 = (bf16[160,1280]{1,0:T(8,128)(2,1)}, f32[128,128]{1,0:T(8,128)}) custom-call(s32[4,20]{1,0:T(4,128)} %owner.1, bf16[256,1280]{1,0:T(8,128)(2,1)} %acts_hbm.1, bf16[256,1280]{1,0:T(8,128)(2,1)} %grads_hbm.1, bf16[160,1280]{1,0:T(8,128)(2,1)} %bitcast.3, bf16[10,128,128]{2,1,0:T(8,128)(2,1)} %qa_hbm.1, bf16[10,128,128]{2,1,0:T(8,128)(2,1)} %qg_hbm.1, ...), custom_call_target="tpu_custom_call" | custom-call | tf_op jit(solution)/shard_map/pallas_call | solution.py:462
  43.1 1.8 %shard_map.87 = (bf16[160,1280]{1,0:T(8,128)(2,1)}, f32[128,128]{1,0:T(8,128)}) custom-call(bf16[160,1280]{1,0:T(8,128)(2,1)} %get-tuple-element.6.update_in, f32[128,128]{1,0:T(8,128)} %get-tuple-element.7.fac_in), custom_call_target="tpu_custom_call" | custom-call | tf_op jit(solution)/shard_map/pallas_call | solution.py:520
